TPU v7x, 256 devices: a whole 4x4x8 slice. The times are simulated.
256 devices in a mesh: dp: 64 (over z, x_lo, y), tensor: 4 (over x_hi, core).
Axes of the slice: x: 4 (x_hi: 2, x_lo: 2; x = x_hi * 2 + x_lo), y: 4, z: 8, core: 2. Of those that a mesh axis runs over, the one named last changes fastest.
Arguments:
- activations: bfloat16 [2, 24576, 4096], P(None, 'dp', 'tensor'), may hold values from -6 to 6
- signals: bfloat16 [3, 24576, 11008], P(None, 'dp', 'tensor'), may hold values from -6 to 6
- projectors: bfloat16 [3, 4096, 128], replicated, may hold values from -0.09375 to 0.09375
- weights: bfloat16 [3, 4096, 11008], P(None, 'dp', 'tensor'), may hold values from -0.09375 to 0.09375
- first_moment: float32 [3, 128, 11008], P(None, 'dp', 'tensor'), may hold values from -0.02734375 to 0.02734375
- second_moment: float32 [3, 128, 11008], P(None, 'dp', 'tensor'), may hold values from 8.138021e-06 to 0.00016276042
Outputs:
- new_weights: bfloat16 [3, 4096, 11008], P(None, 'dp', 'tensor')
- new_first: float32 [3, 128, 11008], P(None, 'dp', 'tensor')
- new_second: float32 [3, 128, 11008], P(None, 'dp', 'tensor')
- direction: float32 [3, 128, 11008], P(None, 'dp', 'tensor')
All inputs are finite; a program needn't handle non-finite values.
Results may differ from a plain program's by a relative error of at most 0.0044.
Values may be sent and summed in bfloat16 or wider, within the bound.
A program may use at most 64 MiB of HBM per device.

v0:
```python
import jax
import jax.numpy as jnp
from jax import lax
from jax.sharding import PartitionSpec as P

beta_one = 0.9
beta_two = 0.999
adam_step = 1000
adam_eps = 1e-08
learning_rate = 0.05
first_fix = 1.0 - beta_one**adam_step
second_fix = 1.0 - beta_two**adam_step


def for_sending(value):
    return jax.tree.map(lambda a: a.astype(jnp.bfloat16) if a.dtype == jnp.float32 else a, value)


def project_block(pieces, projectors):
    contribs = []
    for index, source in enumerate((0, 0, 1)):
        basis_rows = projectors[index]
        contribs.append(jnp.dot(pieces[source], basis_rows, preferred_element_type=jnp.float32))
    return jnp.stack(contribs)


def on_device(activations, signals, projectors, weights, first_moment, second_moment):
    tok_rows = activations.shape[1]
    summed_acts = project_block(
        lax.all_gather(activations, "tensor", axis=2, tiled=True), projectors
    )
    proj_acts = summed_acts.astype(jnp.bfloat16)
    partial_grad = jnp.einsum(
        "ktr,ktf->krf", proj_acts, signals, preferred_element_type=jnp.float32
    )
    count = float(tok_rows * lax.axis_size("dp"))
    own_count = first_moment.shape[1]
    reduced = lax.psum(partial_grad, "dp")
    own_rows = lax.dynamic_slice_in_dim(reduced, lax.axis_index("dp") * own_count, own_count, 1)
    gradient = own_rows / count
    moment_one = beta_one * first_moment + (1.0 - beta_one) * gradient
    moment_two = beta_two * second_moment + (1.0 - beta_two) * gradient * gradient
    heading = moment_one / first_fix / (jnp.sqrt(moment_two / second_fix) + adam_eps)
    weight_rows = weights.shape[1]
    local_basis = lax.dynamic_slice_in_dim(
        projectors, lax.axis_index("dp") * weight_rows, weight_rows, 1
    ).astype(jnp.float32)
    start_change = jnp.zeros((3, weight_rows, weights.shape[2]), jnp.float32)
    pieces = lax.all_gather(for_sending(heading), "dp", axis=1, tiled=True)
    basis_cols = lax.slice_in_dim(local_basis, 0, pieces.shape[1], axis=2)
    change = start_change + jnp.einsum(
        "kdr,krf->kdf", basis_cols, pieces, precision=lax.Precision.HIGHEST
    )
    updated = (weights.astype(jnp.float32) - learning_rate * change).astype(jnp.bfloat16)
    return (updated, moment_one, moment_two, heading)


def solution(mesh):
    placed = (
        P(None, "dp", "tensor"),
        P(None, "dp", "tensor"),
        P(),
        P(None, "dp", "tensor"),
        P(None, "dp", "tensor"),
        P(None, "dp", "tensor"),
    )
    return jax.shard_map(
        on_device,
        mesh=mesh,
        in_specs=placed,
        out_specs=(
            P(None, "dp", "tensor"),
            P(None, "dp", "tensor"),
            P(None, "dp", "tensor"),
            P(None, "dp", "tensor"),
        ),
        check_vma=False,
    )
```

profile of v0, /device:TPU:2, one launch (start us, length us, event | category | flops | bytes accessed | tf_op | source)
XLA Modules:
  0.0 1001.5 jit_solution(16222863340272526812)
XLA Ops:
  7.2 0.0 all-gather.3.cloned.1.call-start
  7.2 0.7 all-gather.3.cloned.1.call-update
  7.9 0.0 all-reduce.2.cloned.1.call-start
  7.9 56.9 %all-gather.3.cloned.1.call-done = bf16[2,384,4096]{2,1,0:T(8,128)(2,1)} async-done(((bf16[2,384,1024]{2,1,0:T(8,128)(2,1)}), bf16[2,384,4096]{2,1,0:T(8,128)(2,1)}) %all-gather.3.cloned.1.call-update) | async-done | bytes 6291472 | tf_op jit(solution)/shard_map/all_gather | solution.py:30
  64.9 0.0 copy-start.3
  64.9 3.3 fusion.9
  68.2 0.7 copy-done.3
  68.9 0.0 slice-start
  68.9 2.4 fusion.10
  71.3 0.0 slice-start.1
  71.3 2.4 fusion.11
  73.6 0.0 slice-done
  73.7 0.0 slice-done.1
  73.7 4.3 fusion.18
  78.0 0.0 copy-start.1
  78.0 0.0 copy-start.2
  78.0 0.0 copy-start
  78.0 0.0 all-reduce.2.cloned.1.call-update
  78.0 0.0 all-gather.5.cloned.1.call-start
  78.1 612.3 %all-reduce.2.cloned.1.call-done = f32[3,128,2752]{2,1,0:T(8,128)} async-done(((f32[3,128,2752]{2,1,0:T(8,128)}), f32[3,128,2752]{2,1,0:T(8,128)}) %all-reduce.2.cloned.1.call-update) | async-done | bytes 4227088 | tf_op jit(solution)/shard_map/psum | solution.py:38
  690.3 0.0 copy-done.1
  690.3 0.0 copy-done.2
  690.3 1.8 fusion.27
  692.2 0.6 copy.12
  692.8 0.0 all-gather.5.cloned.1.call-update
  692.8 298.7 %all-gather.5.cloned.1.call-done = bf16[3,128,2752]{2,0,1:T(4,128)(2,1)} async-done(((bf16[3,2,2752]{2,0,1:T(4,128)(2,1)}), bf16[3,128,2752]{2,0,1:T(4,128)(2,1)}) %all-gather.5.cloned.1.call-update) | async-done | bytes 2113552 | tf_op jit(solution)/shard_map/all_gather | solution.py:49
  991.5 0.0 copy-done
  991.5 3.5 fusion.1
  (1 shorter events, 0.0 us)
Async XLA Ops:
  7.2 57.7 %all-gather.3.cloned.1.call-start = ((), (), s32[]{:S(2)}) async-start(), calls=%async_computation | async-start | bytes 7864320 | tf_op jit(solution)/shard_map/all_gather | solution.py:30
  7.9 682.4 %all-reduce.2.cloned.1.call-start = ((), (), s32[]{:S(2)}) async-start(), calls=%async_computation.1 | async-start | bytes 8650752 | tf_op jit(solution)/shard_map/psum | solution.py:38
  64.9 4.0 copy-start.3
  68.9 4.7 slice-start
  71.3 2.4 slice-start.1
  78.0 612.4 %copy-start.1 = (f32[3,2,2752]{2,1,0:T(2,128)S(1)}, f32[3,2,2752]{2,1,0:T(2,128)}, u32[]{:S(2)}) copy-start(f32[3,2,2752]{2,1,0:T(2,128)} %param.11) | copy-start | bytes 198148
  78.0 612.4 %copy-start.2 = (f32[3,2,2752]{2,1,0:T(2,128)S(1)}, f32[3,2,2752]{2,1,0:T(2,128)}, u32[]{:S(2)}) copy-start(f32[3,2,2752]{2,1,0:T(2,128)} %param.10) | copy-start | bytes 198148
  78.0 913.5 %copy-start = (bf16[3,64,2752]{2,1,0:T(8,128)(2,1)S(1)}, bf16[3,64,2752]{2,1,0:T(8,128)(2,1)}, u32[]{:S(2)}) copy-start(bf16[3,64,2752]{2,1,0:T(8,128)(2,1)} %param.9) | copy-start | bytes 3170308
  78.0 913.5 %all-gather.5.cloned.1.call-start = ((), (), s32[]{:S(2)}) async-start(), calls=%async_computation.2 | async-start | bytes 2928640 | tf_op jit(solution)/shard_map/all_gather | solution.py:49
Sparse Core Ops, SparseCore 0:
  9.8 55.0 all-gather.2
  78.1 612.1 all-reduce.1
  693.0 298.5 all-gather.4
where the time goes:
time: 1010 us; the launch traced here: 1000 us
  waiting for transfers between devices  969 us (96%)
  matrix products  15.8 us (2%)
  between operations  13.8 us (1%)
    psum x1, waiting for transfers between devices, on_device(): reduced = lax.psum(partial_grad, 'dp')  612 us
    all_gather x1, waiting for transfers between devices, on_device(): pieces = lax.all_gather(for_sending(heading), 'dp', axis=1, tiled=True)  299 us
    all_gather x1, waiting for transfers between devices, on_device(): lax.all_gather(activations, 'tensor', axis=2, tiled=True)  56.9 us
  transfers between devices with their start and end apart: 3, of which 3 were waited for; matrix products, arithmetic and copies ran while one was open for 0% of the time, Pallas kernels for 0%

commit v1 on v0

v1 whole, which is shorter than its diff:
```python
import functools

import jax
import jax.numpy as jnp
from jax import lax
from jax.experimental import pallas as pl
from jax.experimental.pallas import tpu as pltpu
from jax.sharding import PartitionSpec as P

MESH = pl.DeviceIdType.MESH
F32, BF16 = jnp.float32, jnp.bfloat16

beta_one = 0.9
beta_two = 0.999
adam_step = 1000
adam_eps = 1e-08
learning_rate = 0.05
first_fix = 1.0 - beta_one**adam_step
second_fix = 1.0 - beta_two**adam_step

NZ, NX, NY = 8, 2, 4
SIZES = {"z": NZ, "y": NY, "x": NX, "xy": NX * NY}
ROUTES = (("z", "xy"), ("y", "x", "z"), ("x", "y", "z"))
BLOCK = 512


def blocks(width):
    return [(at, min(BLOCK, width - at)) for at in range(0, width, BLOCK)]


def route_rows(route):
    return tuple(SIZES[g] for g in route[:-1])


def permutation(route, count):
    p = lax.broadcasted_iota(jnp.int32, (count, count), 0)
    r = lax.broadcasted_iota(jnp.int32, (count, count), 1)
    parts, rest = {}, p // 2
    for g in reversed(route):
        parts[g] = rest % SIZES[g]
        rest = rest // SIZES[g]
    if "xy" in parts:
        parts["x"], parts["y"] = parts["xy"] // NY, parts["xy"] % NY
    natural = ((parts["z"] * NX + parts["x"]) * NY + parts["y"]) * 2 + p % 2
    return (natural == r).astype(F32).astype(BF16)


def kernel(
    act, sig, proj, weights, first, second,
    new_weights, new_first, new_second, new_dir,
    act_v, sig_v, p_v, ploc_v, w_v, m1_v, m2_v, o1_v, o2_v, od_v, wo_v,
    qp, rc, sx, rx, q_v,
    g0, g1, g2, r10, r11, r12, s21, s22, r21, r22, sl, rl, gl, d0, d1, d2,
    lsem, ssem, rsem,
):
    dp, tp = lax.axis_index("dp"), lax.axis_index("tensor")
    z, xl, y = dp // (NX * NY), (dp // NY) % NX, dp % NY
    xh, core = tp // 2, tp % 2
    tokens, depth = act_v.shape[1], act_v.shape[2]
    width = sig_v.shape[1]
    half = tokens // 2
    rows = w_v.shape[1]

    def device(zz, xx, yy, hh=None, cc=None):
        hh = xh if hh is None else hh
        cc = core if cc is None else cc
        return ((zz * NX + xx) * NY + yy, hh * 2 + cc)

    index = {"z": z, "y": y, "x": xl, "xy": xl * NY + y}

    def peer(group, d):
        if group == "z":
            to, frm = (z + d) % NZ, (z + NZ - d) % NZ
            return device(to, xl, y), to, frm
        if group == "y":
            to, frm = (y + d) % NY, (y + NY - d) % NY
            return device(z, xl, to), to, frm
        if group == "x":
            return device(z, 1 - xl, y), 1 - xl, 1 - xl
        dx, dy = d // NY, d % NY
        xx = 1 - xl if dx else xl
        to, frm = (y + dy) % NY, (y + NY - dy) % NY
        return device(z, xx, to), xx * NY + to, xx * NY + frm

    core_peer = device(z, xl, y, xh, 1 - core)
    high_peer = device(z, xl, y, 1 - xh, core)

    loads = {}

    def load(name, src, dst):
        c = pltpu.make_async_copy(src, dst, lsem.at[len(loads)])
        c.start()
        loads[name] = c

    part = pl.ds(pl.multiple_of(tp * depth, depth), depth)
    load("a0", act.at[0], act_v.at[0])
    load("p0", proj.at[0, part], p_v.at[0])
    load("p1", proj.at[1, part], p_v.at[1])
    load("a1", act.at[1], act_v.at[1])
    load("p2", proj.at[2, part], p_v.at[2])
    for k in range(3):
        load(f"s{k}", sig.at[k], sig_v.at[k])
    own = pl.ds(pl.multiple_of(dp * rows, rows), rows)
    load("pl", proj.at[:, own], ploc_v)
    load("m1", first, m1_v)
    load("m2", second, m2_v)
    load("w", weights, w_v)

    barrier = pltpu.get_barrier_semaphore()
    partners = [core_peer, high_peer]
    partners += [peer("z", d)[0] for d in range(1, NZ)]
    partners += [peer("xy", d)[0] for d in range(1, NX * NY)]
    for p in partners:
        pl.semaphore_signal(barrier, inc=1, device_id=p, device_id_type=MESH)

    sends = []

    def remote(src, dst, sem, to):
        return pltpu.make_async_remote_copy(
            src_ref=src, dst_ref=dst, send_sem=ssem.at[sem], recv_sem=rsem.at[sem],
            device_id=to, device_id_type=MESH,
        )

    def send(src, dst, sem, to):
        c = remote(src, dst, sem, to)
        c.start()
        sends.append(c)

    counter = [0]

    def sems(n):
        counter[0] += n
        return counter[0] - n

    core_one, high_one, core_two = sems(3), sems(3), sems(3)

    def project(k):
        source = (0, 0, 1)[k]
        value = jnp.dot(act_v[source], p_v[k], preferred_element_type=F32)
        qp[k] = value.reshape(2, half, value.shape[1])

    for k in range(3):
        if k != 1:
            loads[("a0", "", "a1")[k]].wait()
        loads[f"p{k}"].wait()
        project(k)
        if k == 0:
            pl.semaphore_wait(barrier, len(partners))
        send(qp.at[k, 1 - core], rc.at[k], core_one + k, core_peer)
    for k in range(3):
        remote(qp.at[k, 0], rc.at[k], core_one + k, core_peer).wait_recv()
        total = qp[k, core] + rc[k]
        rc[k] = total
        sx[k] = total.astype(BF16)
        send(sx.at[k], rx.at[k], high_one + k, high_peer)
    for k in range(3):
        remote(sx.at[k], rx.at[k], high_one + k, high_peer).wait_recv()
        q_v[k, core] = (rc[k] + rx[k].astype(F32)).astype(BF16)
        send(q_v.at[k, core], q_v.at[k, core], core_two + k, core_peer)

    grads = (g0, g1, g2)
    firsts = (r10, r11, r12)
    seconds = (None, s21, s22)
    second_recv = (None, r21, r22)
    dirs = (d0, d1, d2)
    perms = [permutation(route, 128) for route in ROUTES]
    base = [[sems(SIZES[g] - 1) for g in route] for route in ROUTES]
    base_back = [[sems(SIZES[g] - 1) for g in route] for route in ROUTES]

    def scatter(k, stage, src, recv):
        group = ROUTES[k][stage]
        for d in range(1, SIZES[group]):
            to, idx, _ = peer(group, d)
            send(src.at[idx], recv.at[d - 1], base[k][stage] + d - 1, to)

    def arrived(k, stage, src, recv):
        group = ROUTES[k][stage]
        for d in range(1, SIZES[group]):
            to, idx, _ = peer(group, d)
            remote(src.at[idx], recv.at[d - 1], base[k][stage] + d - 1, to).wait_recv()

    for k in range(3):
        route = ROUTES[k]
        remote(q_v.at[k, 1 - core], q_v.at[k, 1 - core], core_two + k, core_peer).wait_recv()
        q = q_v[k].reshape(tokens, 128)
        turned = lax.dot_general(
            perms[k], q, (((1,), (1,)), ((), ())), preferred_element_type=F32
        ).astype(BF16)
        loads[f"s{k}"].wait()
        lead = grads[k].shape[:-1]
        for at, w in blocks(width):
            value = lax.dot_general(
                turned, sig_v[k, at : at + w, :], (((1,), (1,)), ((), ())), preferred_element_type=F32
            )
            grads[k][..., at : at + w] = value.astype(BF16).reshape(lead + (w,))
        scatter(k, 0, grads[k], firsts[k])

    def summed(src, recv, idx, at, w):
        total = src[idx, ..., at : at + w].astype(F32)
        for i in range(recv.shape[0]):
            total = total + recv[i, ..., at : at + w].astype(F32)
        return total

    def to_pieces(k, total, at, w):
        for i in range(8):
            sl[k, i, :, at : at + w] = total[2 * i : 2 * i + 2].astype(BF16)

    def first_sum(k):
        route = ROUTES[k]
        arrived(k, 0, grads[k], firsts[k])
        for at, w in blocks(width):
            total = summed(grads[k], firsts[k], index[route[0]], at, w)
            if len(route) == 2:
                to_pieces(k, total, at, w)
            else:
                seconds[k][:, :, at : at + w] = total.astype(BF16)
        if len(route) == 2:
            scatter(k, 1, sl.at[k], rl.at[k])
        else:
            scatter(k, 1, seconds[k], second_recv[k])

    def second_sum(k):
        route = ROUTES[k]
        arrived(k, 1, seconds[k], second_recv[k])
        for at, w in blocks(width):
            to_pieces(k, summed(seconds[k], second_recv[k], index[route[1]], at, w), at, w)
        scatter(k, 2, sl.at[k], rl.at[k])

    outs = []
    count = float(tokens * NZ * NX * NY)

    def store(src, dst):
        c = pltpu.make_async_copy(src, dst, lsem.at[len(loads) + len(outs)])
        c.start()
        outs.append(c)

    def update(k):
        route = ROUTES[k]
        last = len(route) - 1
        arrived(k, last, sl.at[k], rl.at[k])
        idx = index[route[last]]
        for at, w in blocks(width):
            cols = slice(at, at + w)
            gradient = summed(sl.at[k], rl.at[k], idx, at, w) / count
            one = beta_one * m1_v[k, :, cols] + (1.0 - beta_one) * gradient
            two = beta_two * m2_v[k, :, cols] + (1.0 - beta_two) * gradient * gradient
            heading = one / first_fix / (jnp.sqrt(two / second_fix) + adam_eps)
            o1_v[k, :, cols] = one
            o2_v[k, :, cols] = two
            od_v[k, :, cols] = heading
            gl[k, idx, :, cols] = heading.astype(BF16)
        for d in range(1, SIZES[route[last]]):
            to, _, _ = peer(route[last], d)
            send(gl.at[k, idx], gl.at[k, idx], base_back[k][last] + d - 1, to)

    def place(k, stage):
        return tuple(index[g] for g in ROUTES[k][: stage + 1])

    def spread(k, stage):
        group = ROUTES[k][stage]
        at = place(k, stage)
        for d in range(1, SIZES[group]):
            to, _, _ = peer(group, d)
            send(dirs[k].at[at], dirs[k].at[at], base_back[k][stage] + d - 1, to)

    def gathered(k, stage):
        group = ROUTES[k][stage]
        lead = place(k, stage)[:-1]
        for d in range(1, SIZES[group]):
            to, _, frm = peer(group, d)
            slot = dirs[k].at[lead + (frm,)]
            remote(slot, slot, base_back[k][stage] + d - 1, to).wait_recv()

    def joined(k):
        route = ROUTES[k]
        last = len(route) - 1
        for d in range(1, SIZES[route[last]]):
            to, _, frm = peer(route[last], d)
            remote(gl.at[k, frm], gl.at[k, frm], base_back[k][last] + d - 1, to).wait_recv()
        at16 = place(k, last - 1)
        for at, w in blocks(width):
            pieces = [gl[k, i, :, at : at + w].astype(F32) for i in range(8)]
            dirs[k][at16 + (slice(None), slice(at, at + w))] = jnp.concatenate(pieces, axis=0).astype(BF16)
        spread(k, last - 1)

    def finish(k):
        gathered(k, 0)
        basis = lax.dot_general(
            ploc_v[k], perms[k], (((1,), (1,)), ((), ())), preferred_element_type=F32
        ).astype(BF16)
        for at, w in blocks(width):
            cols = slice(at, at + w)
            heading = dirs[k][..., cols].reshape(128, w)
            change = jnp.dot(basis, heading, preferred_element_type=F32)
            wo_v[k, :, cols] = (w_v[k, :, cols].astype(F32) - learning_rate * change).astype(BF16)
        store(wo_v.at[k], new_weights.at[k])

    first_sum(1)
    first_sum(2)
    second_sum(1)
    loads["m1"].wait()
    loads["m2"].wait()
    second_sum(2)
    update(1)
    update(2)
    first_sum(0)
    joined(1)
    joined(2)
    update(0)
    store(o1_v, new_first)
    store(o2_v, new_second)
    store(od_v, new_dir)
    gathered(1, 1)
    spread(1, 0)
    gathered(2, 1)
    spread(2, 0)
    joined(0)
    loads["pl"].wait()
    loads["w"].wait()
    finish(1)
    finish(2)
    finish(0)
    for c in sends:
        c.wait_send()
    for c in outs:
        c.wait()


def on_device(activations, signals, projectors, weights, first_moment, second_moment):
    signals = jnp.transpose(signals, (0, 2, 1))
    _, tokens, depth = activations.shape
    _, width, _ = signals.shape
    rank = projectors.shape[2]
    rows = weights.shape[1]
    half = tokens // 2
    small = first_moment.shape
    vmem = pltpu.VMEM
    lead = [route_rows(r) for r in ROUTES]
    cell = (16, width)

    scratch = [
        vmem(activations.shape, BF16), vmem(signals.shape, BF16), vmem((3, depth, rank), BF16),
        vmem((3, rows, rank), BF16), vmem(weights.shape, BF16), vmem(small, F32), vmem(small, F32),
        vmem(small, F32), vmem(small, F32), vmem(small, F32), vmem(weights.shape, BF16),
        vmem((3, 2, half, rank), F32), vmem((3, half, rank), F32), vmem((3, half, rank), BF16),
        vmem((3, half, rank), BF16), vmem((3, 2, half, rank), BF16),
    ]
    scratch += [vmem(l + cell, BF16) for l in lead]
    scratch += [vmem((l[0] - 1,) + l[1:] + cell, BF16) for l in lead]
    scratch += [vmem(l[1:] + cell, BF16) for l in lead[1:]]
    scratch += [vmem((l[1] - 1,) + cell, BF16) for l in lead[1:]]
    scratch += [
        vmem((3, 8, 2, width), BF16), vmem((3, 7, 2, width), BF16), vmem((3, 8, 2, width), BF16),
    ]
    scratch += [vmem(l + cell, BF16) for l in lead]
    scratch += [
        pltpu.SemaphoreType.DMA((24,)), pltpu.SemaphoreType.DMA((96,)), pltpu.SemaphoreType.DMA((96,)),
    ]
    return pl.pallas_call(
        kernel,
        out_shape=(
            jax.ShapeDtypeStruct(weights.shape, BF16),
            jax.ShapeDtypeStruct(small, F32),
            jax.ShapeDtypeStruct(small, F32),
            jax.ShapeDtypeStruct(small, F32),
        ),
        in_specs=[pl.BlockSpec(memory_space=pl.ANY)] * 6,
        out_specs=(pl.BlockSpec(memory_space=pl.ANY),) * 4,
        scratch_shapes=scratch,
        compiler_params=pltpu.CompilerParams(
            collective_id=0, has_side_effects=True, vmem_limit_bytes=48 << 20
        ),
        name="lowrank_adam",
    )(activations, signals, projectors, weights, first_moment, second_moment)


def solution(mesh):
    split = P(None, "dp", "tensor")
    return jax.shard_map(
        on_device,
        mesh=mesh,
        in_specs=(split, split, P(), split, split, split),
        out_specs=(split, split, split, split),
        check_vma=False,
    )
```

time: 1010 us -> 79.4 us (0.08)
  waiting for transfers between devices: 969 us -> 0 us
  Pallas kernels: 0 us -> 70.3 us
  matrix products: 15.8 us -> 0 us
  between operations: 13.8 us -> 0.65 us
    psum x1 -> x0, waiting for transfers between devices: 612 us -> none  [on_device(): reduced = lax.psum(partial_grad, 'dp')]
    all_gather x2 -> x0, waiting for transfers between devices: 356 us -> none  [the longest x1 299 us: on_device(): pieces = lax.all_gather(for_sending(heading), 'dp', axis=1, tiled=True)]
    pallas_call x0 -> x1, Pallas kernels: none -> 70.3 us  [on_device(): pl.pallas_call(kernel, out_shape=(jax.ShapeDtypeStruct(weights.shape, BF1...]
    dot_general x5 -> x0, matrix products: 15.8 us -> none  [the longest x3 8 us: project_block(): jnp.dot(pieces[source], basis_rows, preferred_element_type=jnp.float32)]
  transfers between devices with their start and end apart: 3 -> 0, of which waited for: 3 -> 0; matrix products, arithmetic and copies ran while one was open for 0% -> 0% of each run, Pallas kernels for 0% -> 0%
where the time goes in v1:
time: 79.4 us; the launch traced here: 78.3 us
  Pallas kernels  70.3 us (89%)
  local copies, waits for them, and re-layouts  7.27 us (9%)
    pallas_call x1, Pallas kernels, on_device(): pl.pallas_call(kernel, out_shape=(jax.ShapeDtypeStruct(weights.shape, BF1...  70.3 us
    unnamed x12, local copies, waits for them, and re-layouts  7.27 us

profile of v1, /device:TPU:2, one launch (start us, length us, event | category | flops | bytes accessed | tf_op | source)
XLA Modules:
  0.0 78.3 jit_solution(4954453054408446877)
XLA Ops:
  0.6 0.0 copy-start
  0.6 1.4 %copy-done = bf16[2,384,1024]{2,1,0:T(8,128)(2,1)S(1)} copy-done((bf16[2,384,1024]{2,1,0:T(8,128)(2,1)S(1)}, bf16[2,384,1024]{2,1,0:T(8,128)(2,1)}, u32[]{:S(2)}) %copy-start) | copy-done | bytes 1572888
  2.0 0.0 copy-start.1
  2.0 1.2 %copy-done.1 = bf16[3,64,2752]{2,1,0:T(8,128)(2,1)S(1)} copy-done((bf16[3,64,2752]{2,1,0:T(8,128)(2,1)S(1)}, bf16[3,64,2752]{2,1,0:T(8,128)(2,1)}, u32[]{:S(2)}) %copy-start.1) | copy-done | bytes 1056792
  3.3 0.0 copy-start.2
  3.3 0.9 %copy-done.2 = f32[3,2,2752]{2,1,0:T(2,128)S(1)} copy-done((f32[3,2,2752]{2,1,0:T(2,128)S(1)}, f32[3,2,2752]{2,1,0:T(2,128)}, u32[]{:S(2)}) %copy-start.2) | copy-done | bytes 66072
  4.2 0.0 copy-start.3
  4.2 0.9 %copy-done.3 = f32[3,2,2752]{2,1,0:T(2,128)S(1)} copy-done((f32[3,2,2752]{2,1,0:T(2,128)S(1)}, f32[3,2,2752]{2,1,0:T(2,128)}, u32[]{:S(2)}) %copy-start.3) | copy-done | bytes 66072
  5.0 70.3 %lowrank_adam.1 = (bf16[3,64,2752]{2,1,0:T(8,128)(2,1)S(1)}, f32[3,2,2752]{2,1,0:T(2,128)S(1)}, f32[3,2,2752]{2,1,0:T(2,128)S(1)}, f32[3,2,2752]{2,1,0:T(2,128)S(1)}) custom-call(bf16[2,384,1024]{2,1,0:T(8,128)(2,1)S(1)} %copy-done, bf16[3,2752,384]{2,1,0:T(8,128)(2,1)} %bitcast.1, bf16[3,4096,128]{2,1,0:T(8,128)(2,1)} %proj.1, ...), custom_call_target="tpu_custom_call" | custom-call | tf_op jit(solution)/shard_map/lowrank_adam/pallas_call | solution.py:359
  75.4 1.0 %copy.14 = bf16[3,64,2752]{2,1,0:T(8,128)(2,1)} copy(bf16[3,64,2752]{2,1,0:T(8,128)(2,1)S(1)} %get-tuple-element.8) | data formatting | bytes 2113536
  76.4 0.6 copy.15
  77.0 0.6 copy.16
  77.6 0.6 copy.17
Async XLA Ops:
  0.6 1.4 %copy-start = (bf16[2,384,1024]{2,1,0:T(8,128)(2,1)S(1)}, bf16[2,384,1024]{2,1,0:T(8,128)(2,1)}, u32[]{:S(2)}) copy-start(bf16[2,384,1024]{2,1,0:T(8,128)(2,1)} %act.1) | copy-start | bytes 4718596
  2.0 1.2 %copy-start.1 = (bf16[3,64,2752]{2,1,0:T(8,128)(2,1)S(1)}, bf16[3,64,2752]{2,1,0:T(8,128)(2,1)}, u32[]{:S(2)}) copy-start(bf16[3,64,2752]{2,1,0:T(8,128)(2,1)} %weights.1) | copy-start | bytes 3170308
  3.3 0.9 %copy-start.2 = (f32[3,2,2752]{2,1,0:T(2,128)S(1)}, f32[3,2,2752]{2,1,0:T(2,128)}, u32[]{:S(2)}) copy-start(f32[3,2,2752]{2,1,0:T(2,128)} %first.1) | copy-start | bytes 198148
  4.2 0.9 %copy-start.3 = (f32[3,2,2752]{2,1,0:T(2,128)S(1)}, f32[3,2,2752]{2,1,0:T(2,128)}, u32[]{:S(2)}) copy-start(f32[3,2,2752]{2,1,0:T(2,128)} %second.1) | copy-start | bytes 198148

commit v2 on v1

v2 whole, which is shorter than its diff:
```python
import functools

import jax
import jax.numpy as jnp
from jax import lax
from jax.experimental import pallas as pl
from jax.experimental.pallas import tpu as pltpu
from jax.sharding import PartitionSpec as P

MESH = pl.DeviceIdType.MESH
F32, BF16 = jnp.float32, jnp.bfloat16

beta_one = 0.9
beta_two = 0.999
adam_step = 1000
adam_eps = 1e-08
learning_rate = 0.05
first_fix = 1.0 - beta_one**adam_step
second_fix = 1.0 - beta_two**adam_step

NZ, NX, NY = 8, 2, 4
SIZES = {"z": NZ, "y": NY, "x": NX, "xy": NX * NY}
AROUND, ACROSS, ALONG = ("z", "xy"), ("y", "x", "z"), ("x", "y", "z")
CUT = 1408
PARTS = (
    (0, 0, ALONG), (0, 1, ACROSS), (1, 0, ALONG), (1, 1, AROUND), (2, 0, ALONG), (2, 1, ACROSS),
)
BLOCK = 512


def span(part, width):
    return (0, CUT) if part[1] == 0 else (CUT, width - CUT)


def blocks(width):
    return [(at, min(BLOCK, width - at)) for at in range(0, width, BLOCK)]


def route_rows(route):
    return tuple(SIZES[g] for g in route[:-1])


def permutation(route, count):
    p = lax.broadcasted_iota(jnp.int32, (count, count), 0)
    r = lax.broadcasted_iota(jnp.int32, (count, count), 1)
    parts, rest = {}, p // 2
    for g in reversed(route):
        parts[g] = rest % SIZES[g]
        rest = rest // SIZES[g]
    if "xy" in parts:
        parts["x"], parts["y"] = parts["xy"] // NY, parts["xy"] % NY
    natural = ((parts["z"] * NX + parts["x"]) * NY + parts["y"]) * 2 + p % 2
    return (natural == r).astype(F32).astype(BF16)


def kernel(
    act, sig, proj, weights, first, second,
    new_weights, new_first, new_second, new_dir,
    act_v, sig_v, p_v, ploc_v, w_v, m1_v, m2_v, qp, rc, sx, rx, q_v, *rest,
):
    n = len(PARTS)
    grads, firsts, seconds, second_recv, sl, rl, gl, dirs = (rest[i * n : (i + 1) * n] for i in range(8))
    lsem, ssem, rsem = rest[8 * n :]
    dp, tp = lax.axis_index("dp"), lax.axis_index("tensor")
    z, xl, y = dp // (NX * NY), (dp // NY) % NX, dp % NY
    xh, core = tp // 2, tp % 2
    tokens, depth = act_v.shape[1], act_v.shape[2]
    width = sig_v.shape[1]
    half = tokens // 2
    rows = w_v.shape[1]

    def device(zz, xx, yy, hh=None, cc=None):
        hh = xh if hh is None else hh
        cc = core if cc is None else cc
        return ((zz * NX + xx) * NY + yy, hh * 2 + cc)

    index = {"z": z, "y": y, "x": xl, "xy": xl * NY + y}

    def peer(group, d):
        if group == "z":
            to, frm = (z + d) % NZ, (z + NZ - d) % NZ
            return device(to, xl, y), to, frm
        if group == "y":
            to, frm = (y + d) % NY, (y + NY - d) % NY
            return device(z, xl, to), to, frm
        if group == "x":
            return device(z, 1 - xl, y), 1 - xl, 1 - xl
        dx, dy = d // NY, d % NY
        xx = 1 - xl if dx else xl
        to, frm = (y + dy) % NY, (y + NY - dy) % NY
        return device(z, xx, to), xx * NY + to, xx * NY + frm

    core_peer = device(z, xl, y, xh, 1 - core)
    high_peer = device(z, xl, y, 1 - xh, core)

    loads = {}

    def load(name, src, dst):
        c = pltpu.make_async_copy(src, dst, lsem.at[len(loads)])
        c.start()
        loads[name] = c

    part = pl.ds(pl.multiple_of(tp * depth, depth), depth)
    load("a0", act.at[0], act_v.at[0])
    load("p0", proj.at[0, part], p_v.at[0])
    load("p1", proj.at[1, part], p_v.at[1])
    load("a1", act.at[1], act_v.at[1])
    load("p2", proj.at[2, part], p_v.at[2])
    for k in range(3):
        load(f"s{k}", sig.at[k], sig_v.at[k])
    own = pl.ds(pl.multiple_of(dp * rows, rows), rows)
    load("pl", proj.at[:, own], ploc_v)
    load("m1", first, m1_v)
    load("m2", second, m2_v)
    load("w", weights, w_v)

    barrier = pltpu.get_barrier_semaphore()
    partners = [core_peer, high_peer]
    partners += [peer("z", d)[0] for d in range(1, NZ)]
    partners += [peer("xy", d)[0] for d in range(1, NX * NY)]
    for p in partners:
        pl.semaphore_signal(barrier, inc=1, device_id=p, device_id_type=MESH)

    sends = []

    def remote(src, dst, sem, to):
        return pltpu.make_async_remote_copy(
            src_ref=src, dst_ref=dst, send_sem=ssem.at[sem], recv_sem=rsem.at[sem],
            device_id=to, device_id_type=MESH,
        )

    def send(src, dst, sem, to):
        c = remote(src, dst, sem, to)
        c.start()
        sends.append(c)

    counter = [0]

    def sems(n):
        counter[0] += n
        return counter[0] - n

    core_one, high_one, core_two = sems(3), sems(3), sems(3)

    def project(k):
        source = (0, 0, 1)[k]
        value = jnp.dot(act_v[source], p_v[k], preferred_element_type=F32)
        qp[k] = value.reshape(2, half, value.shape[1])

    perms = {route: permutation(route, 128) for route in {p[2]: 0 for p in PARTS}}
    base = [[sems(SIZES[g] - 1) for g in p[2]] for p in PARTS]
    base_back = [[sems(SIZES[g] - 1) for g in p[2]] for p in PARTS]

    def core_send(k):
        if k != 1:
            loads[("a0", "", "a1")[k]].wait()
        loads[f"p{k}"].wait()
        project(k)
        if k == 0:
            pl.semaphore_wait(barrier, len(partners))
        send(qp.at[k, 1 - core], rc.at[k], core_one + k, core_peer)

    def high_send(k):
        remote(qp.at[k, 0], rc.at[k], core_one + k, core_peer).wait_recv()
        total = qp[k, core] + rc[k]
        rc[k] = total
        sx[k] = total.astype(BF16)
        send(sx.at[k], rx.at[k], high_one + k, high_peer)

    def core_back(k):
        remote(sx.at[k], rx.at[k], high_one + k, high_peer).wait_recv()
        q_v[k, core] = (rc[k] + rx[k].astype(F32)).astype(BF16)
        send(q_v.at[k, core], q_v.at[k, core], core_two + k, core_peer)

    def scatter(p, stage, src, recv):
        group = PARTS[p][2][stage]
        for d in range(1, SIZES[group]):
            to, idx, _ = peer(group, d)
            send(src.at[idx], recv.at[d - 1], base[p][stage] + d - 1, to)

    def arrived(p, stage, src, recv):
        group = PARTS[p][2][stage]
        for d in range(1, SIZES[group]):
            to, idx, _ = peer(group, d)
            remote(src.at[idx], recv.at[d - 1], base[p][stage] + d - 1, to).wait_recv()

    def gradient_of(k):
        remote(q_v.at[k, 1 - core], q_v.at[k, 1 - core], core_two + k, core_peer).wait_recv()
        q = q_v[k].reshape(tokens, 128)
        loads[f"s{k}"].wait()
        for p, part in enumerate(PARTS):
            if part[0] != k:
                continue
            turned = lax.dot_general(
                perms[part[2]], q, (((1,), (1,)), ((), ())), preferred_element_type=F32
            ).astype(BF16)
            start, size = span(part, width)
            lead = grads[p].shape[:-1]
            for at, w in blocks(size):
                value = lax.dot_general(
                    turned, sig_v[k, start + at : start + at + w, :], (((1,), (1,)), ((), ())),
                    preferred_element_type=F32,
                )
                grads[p][..., at : at + w] = value.astype(BF16).reshape(lead + (w,))
            scatter(p, 0, grads[p], firsts[p])

    def summed(src, recv, idx, at, w):
        total = src[idx, ..., at : at + w].astype(F32)
        for i in range(recv.shape[0]):
            total = total + recv[i, ..., at : at + w].astype(F32)
        return total

    def to_pieces(p, total, at, w):
        for i in range(8):
            sl[p][i, :, at : at + w] = total[2 * i : 2 * i + 2].astype(BF16)

    def first_sum(p):
        route = PARTS[p][2]
        arrived(p, 0, grads[p], firsts[p])
        for at, w in blocks(span(PARTS[p], width)[1]):
            total = summed(grads[p], firsts[p], index[route[0]], at, w)
            if len(route) == 2:
                to_pieces(p, total, at, w)
            else:
                seconds[p][:, :, at : at + w] = total.astype(BF16)
        if len(route) == 2:
            scatter(p, 1, sl[p], rl[p])
        else:
            scatter(p, 1, seconds[p], second_recv[p])

    def second_sum(p):
        route = PARTS[p][2]
        if len(route) == 2:
            return
        arrived(p, 1, seconds[p], second_recv[p])
        for at, w in blocks(span(PARTS[p], width)[1]):
            to_pieces(p, summed(seconds[p], second_recv[p], index[route[1]], at, w), at, w)
        scatter(p, 2, sl[p], rl[p])

    count = float(tokens * NZ * NX * NY)

    def update(p):
        k, _, route = PARTS[p]
        last = len(route) - 1
        arrived(p, last, sl[p], rl[p])
        idx = index[route[last]]
        start, size = span(PARTS[p], width)
        for at, w in blocks(size):
            cols = slice(start + at, start + at + w)
            gradient = summed(sl[p], rl[p], idx, at, w) / count
            one = beta_one * m1_v[k, :, cols] + (1.0 - beta_one) * gradient
            two = beta_two * m2_v[k, :, cols] + (1.0 - beta_two) * gradient * gradient
            heading = one / first_fix / (jnp.sqrt(two / second_fix) + adam_eps)
            new_first[k, :, cols] = one
            new_second[k, :, cols] = two
            new_dir[k, :, cols] = heading
            gl[p][idx, :, at : at + w] = heading.astype(BF16)
        for d in range(1, SIZES[route[last]]):
            to, _, _ = peer(route[last], d)
            send(gl[p].at[idx], gl[p].at[idx], base_back[p][last] + d - 1, to)

    def place(p, stage):
        return tuple(index[g] for g in PARTS[p][2][: stage + 1])

    def spread(p, stage):
        group = PARTS[p][2][stage]
        at = place(p, stage)
        for d in range(1, SIZES[group]):
            to, _, _ = peer(group, d)
            send(dirs[p].at[at], dirs[p].at[at], base_back[p][stage] + d - 1, to)

    def gathered(p, stage):
        group = PARTS[p][2][stage]
        lead = place(p, stage)[:-1]
        for d in range(1, SIZES[group]):
            to, _, frm = peer(group, d)
            slot = dirs[p].at[lead + (frm,)]
            remote(slot, slot, base_back[p][stage] + d - 1, to).wait_recv()

    def joined(p):
        route = PARTS[p][2]
        last = len(route) - 1
        for d in range(1, SIZES[route[last]]):
            to, _, frm = peer(route[last], d)
            remote(gl[p].at[frm], gl[p].at[frm], base_back[p][last] + d - 1, to).wait_recv()
        at16 = place(p, last - 1)
        for at, w in blocks(span(PARTS[p], width)[1]):
            pieces = [gl[p][i, :, at : at + w].astype(F32) for i in range(8)]
            dirs[p][at16 + (slice(None), slice(at, at + w))] = jnp.concatenate(pieces, axis=0).astype(BF16)
        spread(p, last - 1)

    def middle(p):
        if len(PARTS[p][2]) == 3:
            gathered(p, 1)
            spread(p, 0)

    def finish(p):
        k, _, route = PARTS[p]
        gathered(p, 0)
        basis = lax.dot_general(
            ploc_v[k], perms[route], (((1,), (1,)), ((), ())), preferred_element_type=F32
        ).astype(BF16)
        start, size = span(PARTS[p], width)
        for at, w in blocks(size):
            cols = slice(start + at, start + at + w)
            heading = dirs[p][..., at : at + w].reshape(128, w)
            change = jnp.dot(basis, heading, preferred_element_type=F32)
            new_weights[k, :, cols] = (w_v[k, :, cols].astype(F32) - learning_rate * change).astype(BF16)

    for k in range(3):
        core_send(k)
    for k in range(3):
        high_send(k)
    core_back(0)
    core_back(1)
    gradient_of(0)
    core_back(2)
    gradient_of(1)
    gradient_of(2)

    for name in ("m1", "m2", "pl", "w"):
        loads[name].wait()
    order = (0, 1, 2, 4, 5, 3)
    for p in order:
        first_sum(p)
    for p in order:
        second_sum(p)
    for p in order:
        update(p)
    for p in order:
        joined(p)
    for p in order:
        middle(p)
    for p in order:
        finish(p)
    for c in sends:
        c.wait_send()


def write_out(*refs):
    sem = refs[8]
    copies = [pltpu.make_async_copy(refs[i], refs[4 + i], sem.at[i]) for i in range(4)]
    for c in copies:
        c.start()
    for c in copies:
        c.wait()


def on_device(activations, signals, projectors, weights, first_moment, second_moment):
    signals = jnp.transpose(signals, (0, 2, 1))
    _, tokens, depth = activations.shape
    _, width, _ = signals.shape
    rank = projectors.shape[2]
    rows = weights.shape[1]
    half = tokens // 2
    small = first_moment.shape
    vmem = pltpu.VMEM
    lead = [route_rows(p[2]) for p in PARTS]
    cells = [(16, span(p, width)[1]) for p in PARTS]

    def small_like(n):
        return [vmem((n, 2, c[1]), BF16) for c in cells]

    scratch = [
        vmem(activations.shape, BF16), vmem(signals.shape, BF16), vmem((3, depth, rank), BF16),
        vmem((3, rows, rank), BF16), vmem(weights.shape, BF16), vmem(small, F32), vmem(small, F32),
        vmem((3, 2, half, rank), F32), vmem((3, half, rank), F32), vmem((3, half, rank), BF16),
        vmem((3, half, rank), BF16), vmem((3, 2, half, rank), BF16),
    ]
    scratch += [vmem(l + c, BF16) for l, c in zip(lead, cells)]
    scratch += [vmem((l[0] - 1,) + l[1:] + c, BF16) for l, c in zip(lead, cells)]
    scratch += [vmem((l + (1,))[1:2] + c, BF16) for l, c in zip(lead, cells)]
    scratch += [vmem((max((l + (1,))[1] - 1, 1),) + c, BF16) for l, c in zip(lead, cells)]
    scratch += small_like(8) + small_like(7) + small_like(8)
    scratch += [vmem(l + c, BF16) for l, c in zip(lead, cells)]
    scratch += [
        pltpu.SemaphoreType.DMA((32,)), pltpu.SemaphoreType.DMA((160,)), pltpu.SemaphoreType.DMA((160,)),
    ]
    results = ((weights.shape, BF16), (small, F32), (small, F32), (small, F32))
    held = pl.pallas_call(
        kernel,
        out_shape=tuple(vmem(*r) for r in results),
        in_specs=[pl.BlockSpec(memory_space=pltpu.HBM)] * 6,
        out_specs=(pl.BlockSpec(memory_space=vmem),) * 4,
        scratch_shapes=scratch,
        compiler_params=pltpu.CompilerParams(
            collective_id=0, has_side_effects=True, vmem_limit_bytes=60 << 20
        ),
        name="lowrank_adam",
    )(activations, signals, projectors, weights, first_moment, second_moment)
    held = [pltpu.with_memory_space_constraint(h, vmem) for h in held]
    return pl.pallas_call(
        write_out,
        out_shape=tuple(jax.ShapeDtypeStruct(*r) for r in results),
        in_specs=[pl.BlockSpec(memory_space=vmem)] * 4,
        out_specs=(pl.BlockSpec(memory_space=pltpu.HBM),) * 4,
        scratch_shapes=[pltpu.SemaphoreType.DMA((4,))],
        name="write_out",
    )(*held)


def solution(mesh):
    split = P(None, "dp", "tensor")
    return jax.shard_map(
        on_device,
        mesh=mesh,
        in_specs=(split, split, P(), split, split, split),
        out_specs=(split, split, split, split),
        check_vma=False,
    )
```

time: 79.4 us -> 63.4 us (0.80)
  Pallas kernels: 70.3 us -> 62.4 us
  local copies, waits for them, and re-layouts: 7.27 us -> 0 us
    pallas_call x1 -> x2, Pallas kernels: 70.3 us -> 62.4 us  [the longest x1 61.3 us: on_device(): pl.pallas_call(kernel, out_shape=tuple((vmem(*r) for r in results)), in_s...]
    unnamed x12 -> x0, local copies, waits for them, and re-layouts: 7.27 us -> none
where the time goes in v2:
time: 63.4 us; the launch traced here: 63 us
  Pallas kernels  62.4 us (98%)
  between operations  0.64 us (1%)
    pallas_call x1, Pallas kernels, on_device(): pl.pallas_call(kernel, out_shape=tuple((vmem(*r) for r in results)), in_s...  61.3 us

profile of v2, /device:TPU:2, one launch (start us, length us, event | category | flops | bytes accessed | tf_op | source)
XLA Modules:
  0.0 63.0 jit_solution(15953497479273390177)
XLA Ops:
  0.6 61.3 %lowrank_adam.1 = (bf16[3,64,2752]{2,1,0:T(8,128)(2,1)S(1)}, f32[3,2,2752]{2,1,0:T(2,128)S(1)}, f32[3,2,2752]{2,1,0:T(2,128)S(1)}, f32[3,2,2752]{2,1,0:T(2,128)S(1)}) custom-call(bf16[2,384,1024]{2,1,0:T(8,128)(2,1)} %act.1, bf16[3,2752,384]{2,1,0:T(8,128)(2,1)} %bitcast.1, bf16[3,4096,128]{2,1,0:T(8,128)(2,1)} %proj.1, bf16[3,64,2752]{2,1,0:T(8,128)(2,1)} %weights.1, ...), custom_call_target="tpu_custom_call" | custom-call | tf_op jit(solution)/shard_map/lowrank_adam/pallas_call | solution.py:380
  61.9 1.1 %write_out.1 = (bf16[3,64,2752]{2,1,0:T(8,128)(2,1)}, f32[3,2,2752]{2,1,0:T(2,128)}, f32[3,2,2752]{2,1,0:T(2,128)}, f32[3,2,2752]{2,1,0:T(2,128)}) custom-call(bf16[3,64,2752]{2,1,0:T(8,128)(2,1)S(1)} %get-tuple-element.8.refs_0_, f32[3,2,2752]{2,1,0:T(2,128)S(1)} %get-tuple-element.9.refs_1_, f32[3,2,2752]{2,1,0:T(2,128)S(1)} %get-tuple-element.10.refs_2_, ...), custom_call_target="tpu_custom_call" | custom-call | tf_op jit(solution)/shard_map/write_out/pallas_call | solution.py:392

commit v3 on v2

--- a/solution.py
+++ b/solution.py
@@ -21,15 +21,15 @@
 NZ, NX, NY = 8, 2, 4
 SIZES = {"z": NZ, "y": NY, "x": NX, "xy": NX * NY}
 AROUND, ACROSS, ALONG = ("z", "xy"), ("y", "x", "z"), ("x", "y", "z")
-CUT = 1408
 PARTS = (
-    (0, 0, ALONG), (0, 1, ACROSS), (1, 0, ALONG), (1, 1, AROUND), (2, 0, ALONG), (2, 1, ACROSS),
+    (0, 0, 1280, ALONG),
+    (0, 1280, 1472, ACROSS),
+    (1, 0, 1024, ALONG),
+    (1, 1024, 1728, AROUND),
+    (2, 0, 1024, ALONG),
+    (2, 1024, 1728, ACROSS),
 )
 BLOCK = 512
-
-
-def span(part, width):
-    return (0, CUT) if part[1] == 0 else (CUT, width - CUT)
 
 
 def blocks(width):
@@ -104,15 +104,18 @@
     load("a0", act.at[0], act_v.at[0])
     load("p0", proj.at[0, part], p_v.at[0])
     load("p1", proj.at[1, part], p_v.at[1])
-    load("a1", act.at[1], act_v.at[1])
-    load("p2", proj.at[2, part], p_v.at[2])
-    for k in range(3):
-        load(f"s{k}", sig.at[k], sig_v.at[k])
-    own = pl.ds(pl.multiple_of(dp * rows, rows), rows)
-    load("pl", proj.at[:, own], ploc_v)
-    load("m1", first, m1_v)
-    load("m2", second, m2_v)
-    load("w", weights, w_v)
+
+    def load_rest():
+        load("a1", act.at[1], act_v.at[1])
+        load("p2", proj.at[2, part], p_v.at[2])
+        for k in range(3):
+            load(f"s{k}", sig.at[k], sig_v.at[k])
+        own = pl.ds(pl.multiple_of(dp * rows, rows), rows)
+        load("pl", proj.at[:, own], ploc_v)
+        load("m1", first, m1_v)
+        load("m2", second, m2_v)
+        load("w", weights, w_v)
+
 
     barrier = pltpu.get_barrier_semaphore()
     partners = [core_peer, high_peer]
@@ -134,6 +137,11 @@
         c.start()
         sends.append(c)
 
+    def send_all(copies, whole, sem):
+        for src, dst, to in copies:
+            remote(src, dst, sem, to).start()
+        sends.append(remote(whole, whole, sem, copies[0][2]))
+
     counter = [0]
 
     def sems(n):
@@ -147,14 +155,16 @@
         value = jnp.dot(act_v[source], p_v[k], preferred_element_type=F32)
         qp[k] = value.reshape(2, half, value.shape[1])
 
-    perms = {route: permutation(route, 128) for route in {p[2]: 0 for p in PARTS}}
-    base = [[sems(SIZES[g] - 1) for g in p[2]] for p in PARTS]
-    base_back = [[sems(SIZES[g] - 1) for g in p[2]] for p in PARTS]
+    perms = {route: permutation(route, 128) for route in {p[3]: 0 for p in PARTS}}
+    base = [[sems(1) for g in p[3]] for p in PARTS]
+    base_back = [[sems(1) for g in p[3]] for p in PARTS]
 
     def core_send(k):
         if k != 1:
             loads[("a0", "", "a1")[k]].wait()
         loads[f"p{k}"].wait()
+        if k == 0:
+            load_rest()
         project(k)
         if k == 0:
             pl.semaphore_wait(barrier, len(partners))
@@ -172,17 +182,17 @@
         q_v[k, core] = (rc[k] + rx[k].astype(F32)).astype(BF16)
         send(q_v.at[k, core], q_v.at[k, core], core_two + k, core_peer)
 
+    def partners_of(p, stage):
+        group = PARTS[p][3][stage]
+        return [peer(group, d) for d in range(1, SIZES[group])]
+
     def scatter(p, stage, src, recv):
-        group = PARTS[p][2][stage]
-        for d in range(1, SIZES[group]):
-            to, idx, _ = peer(group, d)
-            send(src.at[idx], recv.at[d - 1], base[p][stage] + d - 1, to)
+        copies = [(src.at[idx], recv.at[i], to) for i, (to, idx, _) in enumerate(partners_of(p, stage))]
+        send_all(copies, src.at[pl.ds(0, len(copies))], base[p][stage])
 
     def arrived(p, stage, src, recv):
-        group = PARTS[p][2][stage]
-        for d in range(1, SIZES[group]):
-            to, idx, _ = peer(group, d)
-            remote(src.at[idx], recv.at[d - 1], base[p][stage] + d - 1, to).wait_recv()
+        to = partners_of(p, stage)[0][0]
+        remote(recv, recv, base[p][stage], to).wait_recv()
 
     def gradient_of(k):
         remote(q_v.at[k, 1 - core], q_v.at[k, 1 - core], core_two + k, core_peer).wait_recv()
@@ -192,9 +202,9 @@
             if part[0] != k:
                 continue
             turned = lax.dot_general(
-                perms[part[2]], q, (((1,), (1,)), ((), ())), preferred_element_type=F32
+                perms[part[3]], q, (((1,), (1,)), ((), ())), preferred_element_type=F32
             ).astype(BF16)
-            start, size = span(part, width)
+            start, size = part[1:3]
             lead = grads[p].shape[:-1]
             for at, w in blocks(size):
                 value = lax.dot_general(
@@ -215,9 +225,9 @@
             sl[p][i, :, at : at + w] = total[2 * i : 2 * i + 2].astype(BF16)
 
     def first_sum(p):
-        route = PARTS[p][2]
+        route = PARTS[p][3]
         arrived(p, 0, grads[p], firsts[p])
-        for at, w in blocks(span(PARTS[p], width)[1]):
+        for at, w in blocks(PARTS[p][2]):
             total = summed(grads[p], firsts[p], index[route[0]], at, w)
             if len(route) == 2:
                 to_pieces(p, total, at, w)
@@ -229,22 +239,22 @@
             scatter(p, 1, seconds[p], second_recv[p])
 
     def second_sum(p):
-        route = PARTS[p][2]
+        route = PARTS[p][3]
         if len(route) == 2:
             return
         arrived(p, 1, seconds[p], second_recv[p])
-        for at, w in blocks(span(PARTS[p], width)[1]):
+        for at, w in blocks(PARTS[p][2]):
             to_pieces(p, summed(seconds[p], second_recv[p], index[route[1]], at, w), at, w)
         scatter(p, 2, sl[p], rl[p])
 
     count = float(tokens * NZ * NX * NY)
 
     def update(p):
-        k, _, route = PARTS[p]
+        k, _, _, route = PARTS[p]
         last = len(route) - 1
         arrived(p, last, sl[p], rl[p])
         idx = index[route[last]]
-        start, size = span(PARTS[p], width)
+        start, size = PARTS[p][1:3]
         for at, w in blocks(size):
             cols = slice(start + at, start + at + w)
             gradient = summed(sl[p], rl[p], idx, at, w) / count
@@ -255,62 +265,60 @@
             new_second[k, :, cols] = two
             new_dir[k, :, cols] = heading
             gl[p][idx, :, at : at + w] = heading.astype(BF16)
-        for d in range(1, SIZES[route[last]]):
-            to, _, _ = peer(route[last], d)
-            send(gl[p].at[idx], gl[p].at[idx], base_back[p][last] + d - 1, to)
+        copies = [(gl[p].at[idx], gl[p].at[idx], to) for to, _, _ in partners_of(p, last)]
+        send_all(copies, gl[p].at[pl.ds(0, 7)], base_back[p][last])
 
     def place(p, stage):
-        return tuple(index[g] for g in PARTS[p][2][: stage + 1])
+        return tuple(index[g] for g in PARTS[p][3][: stage + 1])
+
+    def others(p, stage):
+        lead = place(p, stage)[:-1]
+        return dirs[p].at[lead + (pl.ds(0, SIZES[PARTS[p][3][stage]] - 1),)]
 
     def spread(p, stage):
-        group = PARTS[p][2][stage]
-        at = place(p, stage)
-        for d in range(1, SIZES[group]):
-            to, _, _ = peer(group, d)
-            send(dirs[p].at[at], dirs[p].at[at], base_back[p][stage] + d - 1, to)
+        slot = dirs[p].at[place(p, stage)]
+        copies = [(slot, slot, to) for to, _, _ in partners_of(p, stage)]
+        send_all(copies, others(p, stage), base_back[p][stage])
 
     def gathered(p, stage):
-        group = PARTS[p][2][stage]
-        lead = place(p, stage)[:-1]
-        for d in range(1, SIZES[group]):
-            to, _, frm = peer(group, d)
-            slot = dirs[p].at[lead + (frm,)]
-            remote(slot, slot, base_back[p][stage] + d - 1, to).wait_recv()
+        to = partners_of(p, stage)[0][0]
+        remote(others(p, stage), others(p, stage), base_back[p][stage], to).wait_recv()
 
     def joined(p):
-        route = PARTS[p][2]
+        route = PARTS[p][3]
         last = len(route) - 1
-        for d in range(1, SIZES[route[last]]):
-            to, _, frm = peer(route[last], d)
-            remote(gl[p].at[frm], gl[p].at[frm], base_back[p][last] + d - 1, to).wait_recv()
+        seven = gl[p].at[pl.ds(0, 7)]
+        remote(seven, seven, base_back[p][last], partners_of(p, last)[0][0]).wait_recv()
         at16 = place(p, last - 1)
-        for at, w in blocks(span(PARTS[p], width)[1]):
+        for at, w in blocks(PARTS[p][2]):
             pieces = [gl[p][i, :, at : at + w].astype(F32) for i in range(8)]
             dirs[p][at16 + (slice(None), slice(at, at + w))] = jnp.concatenate(pieces, axis=0).astype(BF16)
         spread(p, last - 1)
 
     def middle(p):
-        if len(PARTS[p][2]) == 3:
+        if len(PARTS[p][3]) == 3:
             gathered(p, 1)
             spread(p, 0)
 
     def finish(p):
-        k, _, route = PARTS[p]
+        k, _, _, route = PARTS[p]
         gathered(p, 0)
         basis = lax.dot_general(
             ploc_v[k], perms[route], (((1,), (1,)), ((), ())), preferred_element_type=F32
         ).astype(BF16)
-        start, size = span(PARTS[p], width)
+        start, size = PARTS[p][1:3]
         for at, w in blocks(size):
             cols = slice(start + at, start + at + w)
             heading = dirs[p][..., at : at + w].reshape(128, w)
             change = jnp.dot(basis, heading, preferred_element_type=F32)
             new_weights[k, :, cols] = (w_v[k, :, cols].astype(F32) - learning_rate * change).astype(BF16)
 
-    for k in range(3):
-        core_send(k)
-    for k in range(3):
-        high_send(k)
+    core_send(0)
+    core_send(1)
+    high_send(0)
+    core_send(2)
+    high_send(1)
+    high_send(2)
     core_back(0)
     core_back(1)
     gradient_of(0)
@@ -320,19 +328,15 @@
 
     for name in ("m1", "m2", "pl", "w"):
         loads[name].wait()
-    order = (0, 1, 2, 4, 5, 3)
-    for p in order:
-        first_sum(p)
-    for p in order:
-        second_sum(p)
-    for p in order:
-        update(p)
-    for p in order:
-        joined(p)
-    for p in order:
-        middle(p)
-    for p in order:
-        finish(p)
+    for op, p in (
+        (first_sum, 1), (first_sum, 0), (first_sum, 2), (first_sum, 4), (first_sum, 5), (second_sum, 1),
+        (second_sum, 0), (second_sum, 2), (second_sum, 5), (first_sum, 3), (second_sum, 4), (update, 1),
+        (update, 0), (update, 2), (update, 3), (update, 5), (update, 4), (joined, 0),
+        (joined, 3), (joined, 1), (joined, 2), (joined, 5), (joined, 4), (middle, 1),
+        (middle, 0), (middle, 2), (middle, 5), (middle, 4), (finish, 0), (finish, 2),
+        (finish, 1), (finish, 3), (finish, 4), (finish, 5),
+    ):
+        op(p)
     for c in sends:
         c.wait_send()
 
@@ -355,8 +359,8 @@
     half = tokens // 2
     small = first_moment.shape
     vmem = pltpu.VMEM
-    lead = [route_rows(p[2]) for p in PARTS]
-    cells = [(16, span(p, width)[1]) for p in PARTS]
+    lead = [route_rows(p[3]) for p in PARTS]
+    cells = [(16, p[2]) for p in PARTS]
 
     def small_like(n):
         return [vmem((n, 2, c[1]), BF16) for c in cells]
@@ -373,8 +377,9 @@
     scratch += [vmem((max((l + (1,))[1] - 1, 1),) + c, BF16) for l, c in zip(lead, cells)]
     scratch += small_like(8) + small_like(7) + small_like(8)
     scratch += [vmem(l + c, BF16) for l, c in zip(lead, cells)]
+    n_sem = 9 + 2 * sum(len(p[3]) for p in PARTS)
     scratch += [
-        pltpu.SemaphoreType.DMA((32,)), pltpu.SemaphoreType.DMA((160,)), pltpu.SemaphoreType.DMA((160,)),
+        pltpu.SemaphoreType.DMA((12,)), pltpu.SemaphoreType.DMA((n_sem,)), pltpu.SemaphoreType.DMA((n_sem,)),
     ]
     results = ((weights.shape, BF16), (small, F32), (small, F32), (small, F32))
     held = pl.pallas_call(

time: 63.4 us -> 59.1 us (0.932); the launches traced: 63 us -> 58.1 us
  Pallas kernels: 62.4 us -> 57.4 us
    pallas_call x1, Pallas kernels: 61.3 us -> 56.4 us  [on_device(): pl.pallas_call(kernel, out_shape=tuple((vmem(*r) for r in results)), in_s...]
where the time goes in v3:
time: 59.1 us; the launch traced here: 58.1 us
  Pallas kernels  57.4 us (97%)
  between operations  0.64 us (1%)
    pallas_call x1, Pallas kernels, on_device(): pl.pallas_call(kernel, out_shape=tuple((vmem(*r) for r in results)), in_s...  56.4 us

profile of v3, /device:TPU:2, one launch (start us, length us, event | category | flops | bytes accessed | tf_op | source)
XLA Modules:
  0.0 58.1 jit_solution(4642034075773907662)
XLA Ops:
  0.6 56.4 %lowrank_adam.1 = (bf16[3,64,2752]{2,1,0:T(8,128)(2,1)S(1)}, f32[3,2,2752]{2,1,0:T(2,128)S(1)}, f32[3,2,2752]{2,1,0:T(2,128)S(1)}, f32[3,2,2752]{2,1,0:T(2,128)S(1)}) custom-call(bf16[2,384,1024]{2,1,0:T(8,128)(2,1)} %act.1, bf16[3,2752,384]{2,1,0:T(8,128)(2,1)} %bitcast.1, bf16[3,4096,128]{2,1,0:T(8,128)(2,1)} %proj.1, bf16[3,64,2752]{2,1,0:T(8,128)(2,1)} %weights.1, ...), custom_call_target="tpu_custom_call" | custom-call | tf_op jit(solution)/shard_map/lowrank_adam/pallas_call | solution.py:385
  57.0 1.1 %write_out.1 = (bf16[3,64,2752]{2,1,0:T(8,128)(2,1)}, f32[3,2,2752]{2,1,0:T(2,128)}, f32[3,2,2752]{2,1,0:T(2,128)}, f32[3,2,2752]{2,1,0:T(2,128)}) custom-call(bf16[3,64,2752]{2,1,0:T(8,128)(2,1)S(1)} %get-tuple-element.8.refs_0_, f32[3,2,2752]{2,1,0:T(2,128)S(1)} %get-tuple-element.9.refs_1_, f32[3,2,2752]{2,1,0:T(2,128)S(1)} %get-tuple-element.10.refs_2_, ...), custom_call_target="tpu_custom_call" | custom-call | tf_op jit(solution)/shard_map/write_out/pallas_call | solution.py:397

commit v4 on v3

--- a/solution.py
+++ b/solution.py
@@ -60,7 +60,7 @@
 ):
     n = len(PARTS)
     grads, firsts, seconds, second_recv, sl, rl, gl, dirs = (rest[i * n : (i + 1) * n] for i in range(8))
-    lsem, ssem, rsem = rest[8 * n :]
+    lsem, ssem, rsem, ready = rest[8 * n :]
     dp, tp = lax.axis_index("dp"), lax.axis_index("tensor")
     z, xl, y = dp // (NX * NY), (dp // NY) % NX, dp % NY
     xh, core = tp // 2, tp % 2
@@ -93,6 +93,21 @@
     core_peer = device(z, xl, y, xh, 1 - core)
     high_peer = device(z, xl, y, 1 - xh, core)
 
+    barrier = pltpu.get_barrier_semaphore()
+    along_z = [peer("z", d)[0] for d in (1, NZ - 1)]
+    along_y = [peer("y", d)[0] for d in (1, NY - 1)]
+    partners = [core_peer, high_peer, peer("x", 1)[0]] + along_z + along_y
+    for p in partners:
+        pl.semaphore_signal(barrier, inc=1, device_id=p, device_id_type=MESH)
+    rounds = (along_z + along_y, along_z + along_y, along_z)
+
+    def tell(i):
+        for p in rounds[i]:
+            pl.semaphore_signal(ready.at[i], inc=1, device_id=p, device_id_type=MESH)
+
+    def told(i):
+        pl.semaphore_wait(ready.at[i], len(rounds[i]))
+
     loads = {}
 
     def load(name, src, dst):
@@ -116,13 +131,6 @@
         load("m2", second, m2_v)
         load("w", weights, w_v)
 
-
-    barrier = pltpu.get_barrier_semaphore()
-    partners = [core_peer, high_peer]
-    partners += [peer("z", d)[0] for d in range(1, NZ)]
-    partners += [peer("xy", d)[0] for d in range(1, NX * NY)]
-    for p in partners:
-        pl.semaphore_signal(barrier, inc=1, device_id=p, device_id_type=MESH)
 
     sends = []
 
@@ -314,13 +322,19 @@
             new_weights[k, :, cols] = (w_v[k, :, cols].astype(F32) - learning_rate * change).astype(BF16)
 
     core_send(0)
+    tell(0)
     core_send(1)
     high_send(0)
+    told(0)
+    tell(1)
     core_send(2)
     high_send(1)
     high_send(2)
+    told(1)
+    tell(2)
     core_back(0)
     core_back(1)
+    told(2)
     gradient_of(0)
     core_back(2)
     gradient_of(1)
@@ -380,6 +394,7 @@
     n_sem = 9 + 2 * sum(len(p[3]) for p in PARTS)
     scratch += [
         pltpu.SemaphoreType.DMA((12,)), pltpu.SemaphoreType.DMA((n_sem,)), pltpu.SemaphoreType.DMA((n_sem,)),
+        pltpu.SemaphoreType.REGULAR((3,)),
     ]
     results = ((weights.shape, BF16), (small, F32), (small, F32), (small, F32))
     held = pl.pallas_call(

time: 59.1 us -> 57.4 us (0.971); the launches traced: 58.1 us -> 57.3 us
  Pallas kernels: 57.4 us -> 56.6 us
    pallas_call x1, Pallas kernels: 56.4 us -> 55.5 us  [on_device(): pl.pallas_call(kernel, out_shape=tuple((vmem(*r) for r in results)), in_s...]
where the time goes in v4:
time: 57.4 us; the launch traced here: 57.3 us
  Pallas kernels  56.6 us (99%)
  between operations  0.64 us (1%)
    pallas_call x1, Pallas kernels, on_device(): pl.pallas_call(kernel, out_shape=tuple((vmem(*r) for r in results)), in_s...  55.5 us

profile of v4, /device:TPU:2, one launch (start us, length us, event | category | flops | bytes accessed | tf_op | source)
XLA Modules:
  0.0 57.3 jit_solution(12236514586729506613)
XLA Ops:
  0.6 55.5 %lowrank_adam.1 = (bf16[3,64,2752]{2,1,0:T(8,128)(2,1)S(1)}, f32[3,2,2752]{2,1,0:T(2,128)S(1)}, f32[3,2,2752]{2,1,0:T(2,128)S(1)}, f32[3,2,2752]{2,1,0:T(2,128)S(1)}) custom-call(bf16[2,384,1024]{2,1,0:T(8,128)(2,1)} %act.1, bf16[3,2752,384]{2,1,0:T(8,128)(2,1)} %bitcast.1, bf16[3,4096,128]{2,1,0:T(8,128)(2,1)} %proj.1, bf16[3,64,2752]{2,1,0:T(8,128)(2,1)} %weights.1, ...), custom_call_target="tpu_custom_call" | custom-call | tf_op jit(solution)/shard_map/lowrank_adam/pallas_call | solution.py:400
  56.2 1.1 %write_out.1 = (bf16[3,64,2752]{2,1,0:T(8,128)(2,1)}, f32[3,2,2752]{2,1,0:T(2,128)}, f32[3,2,2752]{2,1,0:T(2,128)}, f32[3,2,2752]{2,1,0:T(2,128)}) custom-call(bf16[3,64,2752]{2,1,0:T(8,128)(2,1)S(1)} %get-tuple-element.8.refs_0_, f32[3,2,2752]{2,1,0:T(2,128)S(1)} %get-tuple-element.9.refs_1_, f32[3,2,2752]{2,1,0:T(2,128)S(1)} %get-tuple-element.10.refs_2_, ...), custom_call_target="tpu_custom_call" | custom-call | tf_op jit(solution)/shard_map/write_out/pallas_call | solution.py:412

commit v5 on v4

--- a/solution.py
+++ b/solution.py
@@ -357,7 +357,8 @@
 
 def write_out(*refs):
     sem = refs[8]
-    copies = [pltpu.make_async_copy(refs[i], refs[4 + i], sem.at[i]) for i in range(4)]
+    copies = [pltpu.make_async_copy(refs[0].at[k], refs[4].at[k], sem.at[3 + k]) for k in range(3)]
+    copies += [pltpu.make_async_copy(refs[i], refs[4 + i], sem.at[i - 1]) for i in range(1, 4)]
     for c in copies:
         c.start()
     for c in copies:
@@ -414,7 +415,7 @@
         out_shape=tuple(jax.ShapeDtypeStruct(*r) for r in results),
         in_specs=[pl.BlockSpec(memory_space=vmem)] * 4,
         out_specs=(pl.BlockSpec(memory_space=pltpu.HBM),) * 4,
-        scratch_shapes=[pltpu.SemaphoreType.DMA((4,))],
+        scratch_shapes=[pltpu.SemaphoreType.DMA((6,))],
         name="write_out",
     )(*held)
 

time: 57.4 us -> 57.4 us (level)
  no operation moved by 1% of the time
where the time goes in v5:
time: 57.4 us; the launch traced here: 57.3 us
  Pallas kernels  56.6 us (99%)
  between operations  0.64 us (1%)
    pallas_call x1, Pallas kernels, on_device(): pl.pallas_call(kernel, out_shape=tuple((vmem(*r) for r in results)), in_s...  55.5 us

profile of v5, /device:TPU:2, one launch (start us, length us, event | category | flops | bytes accessed | tf_op | source)
XLA Modules:
  0.0 57.3 jit_solution(14219821599595357141)
XLA Ops:
  0.6 55.5 %lowrank_adam.1 = (bf16[3,64,2752]{2,1,0:T(8,128)(2,1)S(1)}, f32[3,2,2752]{2,1,0:T(2,128)S(1)}, f32[3,2,2752]{2,1,0:T(2,128)S(1)}, f32[3,2,2752]{2,1,0:T(2,128)S(1)}) custom-call(bf16[2,384,1024]{2,1,0:T(8,128)(2,1)} %act.1, bf16[3,2752,384]{2,1,0:T(8,128)(2,1)} %bitcast.1, bf16[3,4096,128]{2,1,0:T(8,128)(2,1)} %proj.1, bf16[3,64,2752]{2,1,0:T(8,128)(2,1)} %weights.1, ...), custom_call_target="tpu_custom_call" | custom-call | tf_op jit(solution)/shard_map/lowrank_adam/pallas_call | solution.py:401
  56.2 1.1 %write_out.1 = (bf16[3,64,2752]{2,1,0:T(8,128)(2,1)}, f32[3,2,2752]{2,1,0:T(2,128)}, f32[3,2,2752]{2,1,0:T(2,128)}, f32[3,2,2752]{2,1,0:T(2,128)}) custom-call(bf16[3,64,2752]{2,1,0:T(8,128)(2,1)S(1)} %get-tuple-element.8.refs_0_, f32[3,2,2752]{2,1,0:T(2,128)S(1)} %get-tuple-element.9.refs_1_, f32[3,2,2752]{2,1,0:T(2,128)S(1)} %get-tuple-element.10.refs_2_, ...), custom_call_target="tpu_custom_call" | custom-call | tf_op jit(solution)/shard_map/write_out/pallas_call | solution.py:413
